TPU v7x, 32 devices: a whole 2x2x4 slice. The times are simulated.
32 devices in a mesh: bucket: 8 (over z, core), replica: 4 (over y, x).
Axes of the slice: x: 2, y: 2, z: 4, core: 2. Of those that a mesh axis runs over, the one named last changes fastest.
Arguments:
- rows: bfloat16 [32768, 768], P(('bucket', 'replica')), may hold values from -40 to 40, as said below
- cell_ids: int32 [32768, 1], P(('bucket', 'replica')), may hold values from 0 to 15; in each aligned block of 1024 rows (0 to 1023, 1024 to 2047, ...) at most 128 rows name the same one
- start_basis: float32 [16, 768, 768], P('bucket'), may hold values from -0.1 to 1.1, as said below
Outputs:
- rotated: bfloat16 [32768, 768], P(('bucket', 'replica'))
Inputs may be any that keep to these rules, and one draw needn't show every extreme that they name: `cell_ids`: in the rows of one device no cell is named by more than 128 rows, a bound that some block reaches; every cell is named by some row. `rows`: A residual row: a column offset plus rough noise with column and row scales. `start_basis`: the identity plus small dense entries.
All inputs are finite; a program needn't handle non-finite values.
Results may differ from a plain program's by a relative error of at most 0.0049.
Values may be sent and summed in bfloat16 or wider, within the bound.
No kernel may reach another device: no remote copies, remote signals or barrier semaphores. Data moves between devices by JAX's collectives and lax.ppermute only.
A program may use at most 128 MiB of HBM per device.

v0:
```python
import jax
import jax.numpy as jnp
from jax import lax
from jax.sharding import PartitionSpec as P

CELLS = 16
ITERS_NS = 3
CAP = 128


def cell_solve(factor, image):
    return jax.scipy.linalg.solve_triangular(factor, image.T, lower=True).T


def local_gram(image):
    return jnp.einsum("cji,cjk->cik", image, image, precision=lax.Precision.HIGHEST)


def orthonormal(image, gram_matrix):
    factor = jax.vmap(jnp.linalg.cholesky)(gram_matrix)
    return jax.vmap(cell_solve)(factor, image)


def body(rows, cell_ids, start_basis):
    width = rows.shape[1]
    flat_ids = cell_ids[:, 0]
    onehot = (flat_ids[:, None] == jnp.arange(CELLS, dtype=jnp.int32)[None, :]).astype(jnp.int32)
    slot = jnp.sum(jnp.cumsum(onehot, axis=0) * onehot, axis=1) - 1
    send_counts = jnp.sum(onehot, axis=0).astype(jnp.bfloat16)[:, None]
    buffer = jnp.zeros((CELLS, CAP, width), jnp.bfloat16).at[flat_ids, slot].set(rows)
    received, recv_counts = (
        lax.all_to_all(buffer, "bucket", split_axis=0, concat_axis=1, tiled=True),
        lax.all_to_all(send_counts, "bucket", split_axis=0, concat_axis=1, tiled=True),
    )
    count_part = jnp.sum(recv_counts.astype(jnp.float32), axis=1)
    sum_part = jnp.sum(received, axis=1, dtype=jnp.float32)
    square_part = jnp.einsum("crd,cre->cde", received, received, preferred_element_type=jnp.float32)
    count_all, sum_all, square_all = lax.psum((count_part, sum_part, square_part), "replica")
    divisor = jnp.maximum(count_all, 1.0)
    mean = sum_all / divisor[:, None]
    covariance = square_all / divisor[:, None, None] - mean[:, :, None] * mean[:, None, :]
    current = start_basis
    for step in range(ITERS_NS):
        image = jnp.einsum("cij,cjk->cik", covariance, current, precision=lax.Precision.HIGHEST)
        current = orthonormal(image, local_gram(image))
    rotation = current.astype(jnp.bfloat16)
    shift = jnp.einsum(
        "cd,cde->ce", mean, rotation.astype(jnp.float32), precision=lax.Precision.HIGHEST
    )
    product = jnp.einsum("crd,cde->cre", received, rotation, preferred_element_type=jnp.float32)
    rotated_slots = (product - shift[:, None, :]).astype(jnp.bfloat16)
    returned = lax.all_to_all(rotated_slots, "bucket", split_axis=1, concat_axis=0, tiled=True)
    return returned[flat_ids, slot]


def solution(mesh):
    placed = (
        P(("bucket", "replica"), None),
        P(("bucket", "replica"), None),
        P("bucket", None, None),
    )
    return jax.shard_map(
        body, mesh=mesh, in_specs=placed, out_specs=P(("bucket", "replica"), None), check_vma=False
    )
```

profile of v0, /device:TPU:12, one launch (start us, length us, event | category | flops | bytes accessed | tf_op | source)
XLA Modules:
  0.0 1767.4 jit_solution(17684069973694661910)
XLA Ops:
  23.1 74.5 %all_to_all.46 = bf16[16,128,768]{2,1,0:T(8,128)(2,1)S(1)} all-to-all(bf16[16,128,768]{2,1,0:T(8,128)(2,1)} %bitcast.348), channel_id=1, replica_groups=mesh['bucket'=8,'replica'=4] {'bucket'}, dimensions={0} | all-to-all | bytes 6291456 | tf_op jit(solution)/shard_map/all_to_all | solution.py:32
  124.6 93.0 %all-reduce.4.cloned.1.call-done = f32[2,768,768]{2,1,0:T(8,128)} async-done(((f32[2,768,768]{2,1,0:T(8,128)}), f32[2,768,768]{2,1,0:T(8,128)}) %all-reduce.4.cloned.1.call-update) | async-done | bytes 4718608 | tf_op jit(solution)/shard_map/psum | solution.py:38
  217.6 14.6 fusion.194
  234.3 13.4 fusion.199
  260.8 23.5 %custom-call.67 = f32[2,128,128]{2,1,0:T(8,128)S(1)} custom-call(f32[2,128,128]{2,1,0:T(8,128)S(1)} %cholesky.898), custom_call_target="Cholesky" | custom-call | tf_op jit(solution)/shard_map/vmap(jit(cholesky))/cholesky | solution.py:20
  286.7 19.7 %custom-call.68 = f32[2,1,128,128]{2,3,1,0:T(8,128)S(1)} custom-call(f32[2,1,128,128]{3,2,1,0:T(8,128)S(1)} %select_bitcast_fusion.14), custom_call_target="InvertDiagBlocksLowerTriangular" | custom-call | tf_op jit(solution)/shard_map/vmap(jit(cholesky))/cholesky | solution.py:20
  311.0 23.6 %custom-call.69 = f32[2,128,128]{2,1,0:T(8,128)S(1)} custom-call(f32[2,128,128]{2,1,0:T(8,128)S(1)} %cholesky.902), custom_call_target="Cholesky" | custom-call | tf_op jit(solution)/shard_map/vmap(jit(cholesky))/cholesky | solution.py:20
  335.3 19.7 %custom-call.70 = f32[2,1,128,128]{2,3,1,0:T(8,128)S(1)} custom-call(f32[2,1,128,128]{3,2,1,0:T(8,128)S(1)} %get-tuple-element.139), custom_call_target="InvertDiagBlocksLowerTriangular" | custom-call | tf_op jit(solution)/shard_map/vmap(jit(cholesky))/cholesky | solution.py:20
  358.9 23.5 %custom-call.71 = f32[2,128,128]{2,1,0:T(8,128)S(1)} custom-call(f32[2,128,128]{2,1,0:T(8,128)S(1)} %cholesky.907), custom_call_target="Cholesky" | custom-call | tf_op jit(solution)/shard_map/vmap(jit(cholesky))/cholesky | solution.py:20
  383.1 20.1 %custom-call.72 = f32[2,1,128,128]{2,3,1,0:T(8,128)S(1)} custom-call(f32[2,1,128,128]{3,2,1,0:T(8,128)S(1)} %get-tuple-element.137), custom_call_target="InvertDiagBlocksLowerTriangular" | custom-call | tf_op jit(solution)/shard_map/vmap(jit(cholesky))/cholesky | solution.py:20
  407.2 23.5 %custom-call.73 = f32[2,128,128]{2,1,0:T(8,128)S(1)} custom-call(f32[2,128,128]{2,1,0:T(8,128)S(1)} %cholesky.912), custom_call_target="Cholesky" | custom-call | tf_op jit(solution)/shard_map/vmap(jit(cholesky))/cholesky | solution.py:20
  431.4 19.7 %custom-call.74 = f32[2,1,128,128]{2,3,1,0:T(8,128)S(1)} custom-call(f32[2,1,128,128]{3,2,1,0:T(8,128)S(1)} %get-tuple-element.135), custom_call_target="InvertDiagBlocksLowerTriangular" | custom-call | tf_op jit(solution)/shard_map/vmap(jit(cholesky))/cholesky | solution.py:20
  454.7 23.6 %custom-call.75 = f32[2,128,128]{2,1,0:T(8,128)S(1)} custom-call(f32[2,128,128]{2,1,0:T(8,128)S(1)} %cholesky.917), custom_call_target="Cholesky" | custom-call | tf_op jit(solution)/shard_map/vmap(jit(cholesky))/cholesky | solution.py:20
  479.0 19.7 %custom-call.76 = f32[2,1,128,128]{2,3,1,0:T(8,128)S(1)} custom-call(f32[2,1,128,128]{3,2,1,0:T(8,128)S(1)} %get-tuple-element.133), custom_call_target="InvertDiagBlocksLowerTriangular" | custom-call | tf_op jit(solution)/shard_map/vmap(jit(cholesky))/cholesky | solution.py:20
  501.9 23.5 %custom-call.77 = f32[2,128,128]{2,1,0:T(8,128)S(1)} custom-call(f32[2,128,128]{2,1,0:T(8,128)S(1)} %convolution_subtract_fusion.20), custom_call_target="Cholesky" | custom-call | tf_op jit(solution)/shard_map/vmap(jit(cholesky))/cholesky | solution.py:20
  531.9 17.9 %while.6 = (s32[]{:T(128)}, f32[2,768,768]{2,1,0:T(8,128)}, s32[6,2]{0,1:T(2,128)S(1)}, f32[6,2,128,128]{3,2,0,1:T(8,128)S(1)}, s32[]{:T(128)}) while((s32[]{:T(128)}, f32[2,768,768]{2,1,0:T(8,128)}, s32[6,2]{0,1:T(2,128)S(1)}, f32[6,2,128,128]{3,2,0,1:T(8,128)S(1)}, s32[]{:T(128)}) %tuple.117), condition=%wide.while_cond, body=%wide.while_body.sunk | while | flops 2 | bytes 262253 | solution.py:12
  549.8 118.3 %custom-call.78 = f32[2,6,128,128]{2,3,1,0:T(8,128)S(1)} custom-call(f32[2,6,128,128]{3,2,1,0:T(8,128)S(1)} %bitcast.353), custom_call_target="InvertDiagBlocksLowerTriangular" | custom-call | tf_op jit(solution)/shard_map/vmap(jit(_solve_triangular))/triangular_solve | solution.py:12
  715.3 13.8 fusion.200
  741.8 23.5 %custom-call.79 = f32[2,128,128]{2,1,0:T(8,128)S(1)} custom-call(f32[2,128,128]{2,1,0:T(8,128)S(1)} %cholesky.921), custom_call_target="Cholesky" | custom-call | tf_op jit(solution)/shard_map/vmap(jit(cholesky))/cholesky | solution.py:20
  767.7 19.8 %custom-call.80 = f32[2,1,128,128]{2,3,1,0:T(8,128)S(1)} custom-call(f32[2,1,128,128]{3,2,1,0:T(8,128)S(1)} %select_bitcast_fusion.9), custom_call_target="InvertDiagBlocksLowerTriangular" | custom-call | tf_op jit(solution)/shard_map/vmap(jit(cholesky))/cholesky | solution.py:20
  792.1 23.5 %custom-call.81 = f32[2,128,128]{2,1,0:T(8,128)S(1)} custom-call(f32[2,128,128]{2,1,0:T(8,128)S(1)} %cholesky.925), custom_call_target="Cholesky" | custom-call | tf_op jit(solution)/shard_map/vmap(jit(cholesky))/cholesky | solution.py:20
  816.2 19.7 %custom-call.82 = f32[2,1,128,128]{2,3,1,0:T(8,128)S(1)} custom-call(f32[2,1,128,128]{3,2,1,0:T(8,128)S(1)} %get-tuple-element.130), custom_call_target="InvertDiagBlocksLowerTriangular" | custom-call | tf_op jit(solution)/shard_map/vmap(jit(cholesky))/cholesky | solution.py:20
  839.8 23.7 %custom-call.83 = f32[2,128,128]{2,1,0:T(8,128)S(1)} custom-call(f32[2,128,128]{2,1,0:T(8,128)S(1)} %cholesky.930), custom_call_target="Cholesky" | custom-call | tf_op jit(solution)/shard_map/vmap(jit(cholesky))/cholesky | solution.py:20
  864.2 19.7 %custom-call.84 = f32[2,1,128,128]{2,3,1,0:T(8,128)S(1)} custom-call(f32[2,1,128,128]{3,2,1,0:T(8,128)S(1)} %get-tuple-element.128), custom_call_target="InvertDiagBlocksLowerTriangular" | custom-call | tf_op jit(solution)/shard_map/vmap(jit(cholesky))/cholesky | solution.py:20
  887.9 23.5 %custom-call.85 = f32[2,128,128]{2,1,0:T(8,128)S(1)} custom-call(f32[2,128,128]{2,1,0:T(8,128)S(1)} %cholesky.935), custom_call_target="Cholesky" | custom-call | tf_op jit(solution)/shard_map/vmap(jit(cholesky))/cholesky | solution.py:20
  912.1 20.1 %custom-call.86 = f32[2,1,128,128]{2,3,1,0:T(8,128)S(1)} custom-call(f32[2,1,128,128]{3,2,1,0:T(8,128)S(1)} %get-tuple-element.126), custom_call_target="InvertDiagBlocksLowerTriangular" | custom-call | tf_op jit(solution)/shard_map/vmap(jit(cholesky))/cholesky | solution.py:20
  935.8 23.5 %custom-call.87 = f32[2,128,128]{2,1,0:T(8,128)S(1)} custom-call(f32[2,128,128]{2,1,0:T(8,128)S(1)} %cholesky.940), custom_call_target="Cholesky" | custom-call | tf_op jit(solution)/shard_map/vmap(jit(cholesky))/cholesky | solution.py:20
  960.0 19.7 %custom-call.88 = f32[2,1,128,128]{2,3,1,0:T(8,128)S(1)} custom-call(f32[2,1,128,128]{3,2,1,0:T(8,128)S(1)} %get-tuple-element.124), custom_call_target="InvertDiagBlocksLowerTriangular" | custom-call | tf_op jit(solution)/shard_map/vmap(jit(cholesky))/cholesky | solution.py:20
  982.8 23.6 %custom-call.89 = f32[2,128,128]{2,1,0:T(8,128)S(1)} custom-call(f32[2,128,128]{2,1,0:T(8,128)S(1)} %convolution_subtract_fusion.19), custom_call_target="Cholesky" | custom-call | tf_op jit(solution)/shard_map/vmap(jit(cholesky))/cholesky | solution.py:20
  1013.3 17.9 %while.7 = (s32[]{:T(128)}, f32[2,768,768]{2,1,0:T(8,128)}, s32[6,2]{0,1:T(2,128)S(1)}, f32[6,2,128,128]{3,2,0,1:T(8,128)S(1)}, s32[]{:T(128)}) while((s32[]{:T(128)}, f32[2,768,768]{2,1,0:T(8,128)}, s32[6,2]{0,1:T(2,128)S(1)}, f32[6,2,128,128]{3,2,0,1:T(8,128)S(1)}, s32[]{:T(128)}) %tuple.128), condition=%wide.while_cond.clone, body=%wide.while_body.clone.sunk | while | flops 2 | bytes 262253 | solution.py:12
  1031.1 118.1 %custom-call.90 = f32[2,6,128,128]{2,3,1,0:T(8,128)S(1)} custom-call(f32[2,6,128,128]{3,2,1,0:T(8,128)S(1)} %bitcast.354), custom_call_target="InvertDiagBlocksLowerTriangular" | custom-call | tf_op jit(solution)/shard_map/vmap(jit(_solve_triangular))/triangular_solve | solution.py:12
  1182.6 11.8 fusion.192
  1196.6 13.6 fusion.201
  1222.7 23.5 %custom-call.91 = f32[2,128,128]{2,1,0:T(8,128)S(1)} custom-call(f32[2,128,128]{2,1,0:T(8,128)S(1)} %cholesky.944), custom_call_target="Cholesky" | custom-call | tf_op jit(solution)/shard_map/vmap(jit(cholesky))/cholesky | solution.py:20
  1248.8 20.1 %custom-call.92 = f32[2,1,128,128]{2,3,1,0:T(8,128)S(1)} custom-call(f32[2,1,128,128]{3,2,1,0:T(8,128)S(1)} %select_bitcast_fusion.4), custom_call_target="InvertDiagBlocksLowerTriangular" | custom-call | tf_op jit(solution)/shard_map/vmap(jit(cholesky))/cholesky | solution.py:20
  1273.3 23.5 %custom-call.93 = f32[2,128,128]{2,1,0:T(8,128)S(1)} custom-call(f32[2,128,128]{2,1,0:T(8,128)S(1)} %cholesky.948), custom_call_target="Cholesky" | custom-call | tf_op jit(solution)/shard_map/vmap(jit(cholesky))/cholesky | solution.py:20
  1297.5 19.7 %custom-call.94 = f32[2,1,128,128]{2,3,1,0:T(8,128)S(1)} custom-call(f32[2,1,128,128]{3,2,1,0:T(8,128)S(1)} %get-tuple-element.121), custom_call_target="InvertDiagBlocksLowerTriangular" | custom-call | tf_op jit(solution)/shard_map/vmap(jit(cholesky))/cholesky | solution.py:20
  1321.2 23.6 %custom-call.95 = f32[2,128,128]{2,1,0:T(8,128)S(1)} custom-call(f32[2,128,128]{2,1,0:T(8,128)S(1)} %cholesky.953), custom_call_target="Cholesky" | custom-call | tf_op jit(solution)/shard_map/vmap(jit(cholesky))/cholesky | solution.py:20
  1345.5 19.7 %custom-call.96 = f32[2,1,128,128]{2,3,1,0:T(8,128)S(1)} custom-call(f32[2,1,128,128]{3,2,1,0:T(8,128)S(1)} %get-tuple-element.119), custom_call_target="InvertDiagBlocksLowerTriangular" | custom-call | tf_op jit(solution)/shard_map/vmap(jit(cholesky))/cholesky | solution.py:20
  1369.2 23.5 %custom-call.97 = f32[2,128,128]{2,1,0:T(8,128)S(1)} custom-call(f32[2,128,128]{2,1,0:T(8,128)S(1)} %cholesky.958), custom_call_target="Cholesky" | custom-call | tf_op jit(solution)/shard_map/vmap(jit(cholesky))/cholesky | solution.py:20
  1393.4 19.9 %custom-call.98 = f32[2,1,128,128]{2,3,1,0:T(8,128)S(1)} custom-call(f32[2,1,128,128]{3,2,1,0:T(8,128)S(1)} %get-tuple-element.117), custom_call_target="InvertDiagBlocksLowerTriangular" | custom-call | tf_op jit(solution)/shard_map/vmap(jit(cholesky))/cholesky | solution.py:20
  1416.9 23.5 %custom-call.99 = f32[2,128,128]{2,1,0:T(8,128)S(1)} custom-call(f32[2,128,128]{2,1,0:T(8,128)S(1)} %cholesky.963), custom_call_target="Cholesky" | custom-call | tf_op jit(solution)/shard_map/vmap(jit(cholesky))/cholesky | solution.py:20
  1441.1 19.7 %custom-call.100 = f32[2,1,128,128]{2,3,1,0:T(8,128)S(1)} custom-call(f32[2,1,128,128]{3,2,1,0:T(8,128)S(1)} %get-tuple-element.115), custom_call_target="InvertDiagBlocksLowerTriangular" | custom-call | tf_op jit(solution)/shard_map/vmap(jit(cholesky))/cholesky | solution.py:20
  1463.8 23.9 %custom-call.101 = f32[2,128,128]{2,1,0:T(8,128)S(1)} custom-call(f32[2,128,128]{2,1,0:T(8,128)S(1)} %convolution_subtract_fusion.18), custom_call_target="Cholesky" | custom-call | tf_op jit(solution)/shard_map/vmap(jit(cholesky))/cholesky | solution.py:20
  1494.5 18.0 %while.8 = (s32[]{:T(128)}, f32[2,768,768]{2,1,0:T(8,128)}, s32[6,2]{0,1:T(2,128)S(1)}, f32[6,2,128,128]{3,2,0,1:T(8,128)S(1)}, s32[]{:T(128)}) while((s32[]{:T(128)}, f32[2,768,768]{2,1,0:T(8,128)}, s32[6,2]{0,1:T(2,128)S(1)}, f32[6,2,128,128]{3,2,0,1:T(8,128)S(1)}, s32[]{:T(128)}) %tuple.129), condition=%wide.while_cond.clone.1, body=%wide.while_body.clone.1.sunk | while | flops 2 | bytes 262253 | solution.py:12
  1512.4 118.1 %custom-call.102 = f32[2,6,128,128]{2,3,1,0:T(8,128)S(1)} custom-call(f32[2,6,128,128]{3,2,1,0:T(8,128)S(1)} %bitcast.352), custom_call_target="InvertDiagBlocksLowerTriangular" | custom-call | tf_op jit(solution)/shard_map/vmap(jit(_solve_triangular))/triangular_solve | solution.py:12
  1671.5 74.1 %all_to_all.47 = bf16[2,1024,768]{2,0,1:T(2,128)(2,1)S(1)} all-to-all(bf16[2,1024,768]{2,0,1:T(2,128)(2,1)S(1)} %copy.347), channel_id=1, replica_groups=mesh['bucket'=8,'replica'=4] {'bucket'}, dimensions={1} | all-to-all | bytes 6291456 | tf_op jit(solution)/shard_map/all_to_all | solution.py:52
  1746.1 13.9 gather_fusion
  (266 shorter events, 354.9 us)
Async XLA Ops:
  6.5 211.0 %all-reduce.4.cloned.1.call-start = ((), (), s32[]{:S(2)}) async-start(), calls=%async_computation.3 | async-start | bytes 9437184 | tf_op jit(solution)/shard_map/psum | solution.py:38
  97.8 1.7 copy-start.7
  104.6 9.7 all-to-all-start.1
  232.2 2.2 copy-start.1
  258.6 2.2 copy-start.4
  403.1 123.4 %copy-start.6 = (pred[768,768]{1,0:T(8,128)(4,1)S(1)}, pred[768,768]{1,0:T(8,128)(4,1)}, u32[]{:S(2)}) copy-start(pred[768,768]{1,0:T(8,128)(4,1)} %iota_compare_fusion) | copy-start | bytes 1769476
  668.1 10.7 slice-start.2
  672.9 5.8 slice-start.3
  691.2 10.0 slice-start.6
  692.1 9.1 slice-start.7
  713.1 2.2 copy-start.2
  739.5 2.2 copy-start.5
  1149.3 10.7 slice-start.4
  1154.1 5.8 slice-start.5
  1172.6 10.0 slice-start.8
  1173.5 9.1 slice-start.9
  1194.4 2.1 copy-start
  1220.5 2.2 copy-start.3
  1630.5 10.6 slice-start
  1635.3 5.8 slice-start.1
  1654.5 10.9 copy-start.8
Sparse Core Ops, SparseCore 0:
  104.0 113.4 all-reduce.3
where the time goes:
time: 1780 us; the launch traced here: 1770 us
  other arithmetic  1130 us (63%)
  matrix products  245 us (14%)
  blocking collectives  158 us (9%)
  local copies, waits for them, and re-layouts  121 us (7%)
  waiting for transfers between devices  96.1 us (5%)
    another operation x71, other arithmetic, orthonormal(): factor = jax.vmap(jnp.linalg.cholesky)(gram_matrix)  733 us
    another operation x8, other arithmetic, cell_solve(): return jax.scipy.linalg.solve_triangular(factor, image.T, lower=True).T  371 us
    another operation x33, matrix products, cell_solve(): return jax.scipy.linalg.solve_triangular(factor, image.T, lower=True).T  98.8 us
    psum x1, waiting for transfers between devices, body(): lax.psum((count_part, sum_part, square_part), 'replica')  93 us
    all_to_all x1, blocking collectives, body(): lax.all_to_all(buffer, 'bucket', split_axis=0, concat_axis=1, tiled=True)  74.5 us
    all_to_all x1, blocking collectives, body(): lax.all_to_all(rotated_slots, 'bucket', split_axis=1, concat_axis=0, tile...  74.1 us
    another operation x30, matrix products, orthonormal(): factor = jax.vmap(jnp.linalg.cholesky)(gram_matrix)  57.8 us
    another operation x58, local copies, waits for them, and re-layouts, cell_solve(): return jax.scipy.linalg.solve_triangular(factor, image.T, lower=True).T  53.5 us
  transfers between devices with their start and end apart: 2, of which 2 were waited for; matrix products, arithmetic and copies ran while one was open for 0% of the time, Pallas kernels for 0%

commit v1 on v0

v1 whole, which is shorter than its diff:
```python
import functools
import jax
import jax.numpy as jnp
from jax import lax
from jax.experimental import pallas as pl
from jax.experimental.pallas import tpu as pltpu
from jax.sharding import Mesh, PartitionSpec as P

CELLS = 16
ITERS_NS = 3
CAP = 128
BLK = 128
SUB = 16
WIDE = 256
PAD_MARK = 128.0
F32 = jnp.float32
BF16 = jnp.bfloat16
NT = (((1,), (1,)), ((), ()))
VMEM_LIMIT = 56 * 1024 * 1024


def split(value):
    high = value.astype(BF16)
    return high, (value - high.astype(F32)).astype(BF16)


def dot(left, right):
    return jnp.dot(left, right, preferred_element_type=F32)


def dot_nt(left, right):
    return lax.dot_general(left, right, NT, preferred_element_type=F32)


def product(left, right, multiply=dot):
    high, low = left
    size = high.shape[0]
    both = multiply(jnp.concatenate([high, low], axis=0), right[0])
    return both[:size, :] + (both[size:, :] + multiply(high, right[1]))


def inverse_factors(squares):
    steps = BLK // SUB
    chains = range(len(squares))
    lane = lax.broadcasted_iota(jnp.int32, (SUB, BLK), 1)
    line = lax.broadcasted_iota(jnp.int32, (SUB, BLK), 0)
    even = lax.broadcasted_iota(jnp.int32, (SUB, 2 * BLK), 0) % 2 == 0
    parts = [[square[SUB * b : SUB * (b + 1), :] for b in range(steps)] for square in squares]
    units = [[(lane == line + SUB * b).astype(F32) for b in range(steps)] for _ in chains]
    done = [[] for _ in chains]

    def begin(n, b):
        row, carry = parts[n][b], units[n][b]
        first = SUB * b
        column = [
            jnp.broadcast_to(row[:, first + k : first + k + 1], (SUB, BLK)) for k in range(SUB)
        ]
        zeros = jnp.zeros((SUB, BLK), F32)
        return dict(
            column=column, row=row, carry=carry, forward=carry, pivots=zeros, alpha=zeros, beta=zeros
        )

    def advance(state, k):
        q = k + 1
        column = state["column"]
        one, two = column[k], column[q]
        head, side = one[k : k + 1, :], one[q : q + 1, :]
        cross, tail = two[k : k + 1, :], two[q : q + 1, :]
        det = head * tail - cross * side
        inverse = 1.0 / det
        pair = (line == k) | (line == q)
        ratio_one = jnp.where(pair, 0.0, one * tail - two * side) * inverse
        ratio_two = jnp.where(pair, 0.0, two * head - one * cross) * inverse

        def clear(value, left, right):
            return value - (left * value[k : k + 1, :] + right * value[q : q + 1, :])

        for j in range(k + 2, SUB):
            column[j] = clear(column[j], ratio_one, ratio_two)
        state["row"] = clear(state["row"], ratio_one, ratio_two)
        state["carry"] = clear(state["carry"], ratio_one, ratio_two)
        single = 1.0 / head
        low_one = jnp.where(line > q, ratio_one, jnp.where(line == q, side * single, 0.0))
        low_two = jnp.where(line > q, ratio_two, 0.0)
        state["forward"] = clear(state["forward"], low_one, low_two)

        def keep(name, upper, lower):
            state[name] = jnp.where(line == k, upper, jnp.where(line == q, lower, state[name]))

        keep("pivots", head, det * single)
        keep("alpha", tail * inverse, head * inverse)
        keep("beta", -cross * inverse, -side * inverse)

    def finish(n, b, state):
        done[n].append(state["forward"] * lax.rsqrt(state["pivots"]))
        if b + 1 == steps:
            return
        part, unit = parts[n], units[n]
        rest = jnp.concatenate(part[b + 1 :], axis=0)
        place = (lax.broadcasted_iota(jnp.int32, rest.shape, 1) - SUB * b) % BLK // SUB
        high = rest.astype(BF16).astype(F32)
        low = rest - high
        terms = jnp.where(place == 0, high, 0.0)
        terms = jnp.where(place == 1, pltpu.roll(low, SUB, 1), terms)
        terms = jnp.where(place == 2, pltpu.roll(high, 2 * SUB, 1), terms).astype(BF16)
        both = jnp.concatenate([state["row"], state["carry"]], axis=1)
        swapped = jnp.where(even, pltpu.roll(both, SUB - 1, 0), pltpu.roll(both, 1, 0))
        alpha = jnp.concatenate([state["alpha"]] * 2, axis=1)
        beta = jnp.concatenate([state["beta"]] * 2, axis=1)
        both_high, both_low = split(alpha * both + beta * swapped)
        filled = [jnp.zeros((SUB, 2 * BLK), BF16)] * steps
        filled[b] = both_high
        filled[(b + 1) % steps] = both_high
        filled[(b + 2) % steps] = both_low
        update = dot(terms, jnp.concatenate(filled, axis=0))
        for i in range(b + 1, steps):
            at = SUB * (i - b - 1)
            part[i] = part[i] - update[at : at + SUB, :BLK]
            unit[i] = unit[i] - update[at : at + SUB, BLK:]

    for b in range(steps):
        states = [begin(n, b) for n in chains]
        for k in range(0, SUB, 2):
            for state in states:
                advance(state, k)
        for n in chains:
            finish(n, b, states[n])
    return [jnp.concatenate(pieces, axis=0) for pieces in done]


def inverse_factors_wide(squares):
    firsts = inverse_factors([square[:BLK, :BLK] for square in squares])
    terms = [split(first) for first in firsts]
    factors = [
        split(product(split(square[BLK:, :BLK]), term, dot_nt))
        for square, term in zip(squares, terms)
    ]
    seconds = inverse_factors(
        [
            square[BLK:, BLK:] - product(factor, factor, dot_nt)
            for square, factor in zip(squares, factors)
        ]
    )
    results = []
    for first, term, factor, second in zip(firsts, terms, factors, seconds):
        corner = product(split(second), split(product(factor, term)))
        upper = jnp.concatenate([first, jnp.zeros((BLK, BLK), F32)], axis=1)
        results.append(
            jnp.concatenate([upper, jnp.concatenate([-corner, second], axis=1)], axis=0)
        )
    return results


FIRST, SECOND = slice(0, WIDE), slice(WIDE, 2 * WIDE)


def terms_of(ref):
    return ref[FIRST, :], ref[SECOND, :]


def wave(cov_ref, tasks):
    width = cov_ref.shape[1]
    images, grams = [], []
    for source, before_refs, _ in tasks:
        image = product(source, (cov_ref[:width, :], cov_ref[width:, :]))
        if before_refs:
            image_terms = split(image)
            for before_ref in before_refs:
                before = terms_of(before_ref)
                along = split(product(image_terms, before, dot_nt))
                image = image - product(along, before)
        image_terms = split(image)
        images.append(image_terms)
        grams.append(product(image_terms, image_terms, dot_nt))
    for inverse, image_terms, task in zip(inverse_factors_wide(grams), images, tasks):
        high, low = split(product(split(inverse), image_terms))
        task[2][FIRST, :] = high
        task[2][SECOND, :] = low


def rotate(mean, rows_ref, rotation, out_ref, columns):
    width = mean.shape[1]
    high = mean.astype(BF16)
    left = mean - high.astype(F32)
    middle = left.astype(BF16)
    low = (left - middle.astype(F32)).astype(BF16)
    pieces = jnp.concatenate([high, middle, low, jnp.zeros((13, width), BF16)], axis=0)
    shift = jnp.sum(dot_nt(pieces, rotation), axis=0, keepdims=True)
    some = 512
    for n in range(rows_ref.shape[0] // some):
        at = slice(some * n, some * (n + 1))
        out_ref[at, columns] = (dot_nt(rows_ref[at, :], rotation) - shift).astype(BF16)


def first_kernel(
    moments_ref, moments_other_ref, start_ref, rows_hbm_ref,
    out_ref, cov_ref, mean_ref, q20_ref, q30_ref, q21_ref, q12_ref,
    rows_ref, q10_ref, q11_ref, sem,
):
    copy = pltpu.make_async_copy(rows_hbm_ref, rows_ref, sem)
    copy.start()
    width = cov_ref.shape[1]
    tail = moments_ref[width : width + 8, :] + moments_other_ref[width : width + 8, :]
    divisor = jnp.maximum(tail[1:2, :], 1.0)
    mean = tail[0:1, :] / divisor
    mean_rows = jnp.broadcast_to(mean, (BLK, width))
    for i in range(width // BLK):
        at = slice(BLK * i, BLK * (i + 1))
        mean_column = jnp.broadcast_to(mean_rows[:, at].T[:, :1], (BLK, width))
        square = moments_ref[at, :] + moments_other_ref[at, :]
        high, low = split(square / divisor - mean_column * mean)
        cov_ref[BLK * i : BLK * (i + 1), :] = high
        cov_ref[width + BLK * i : width + BLK * (i + 1), :] = low
    mean_ref[...] = jnp.broadcast_to(mean, mean_ref.shape)

    def start(i):
        return split(start_ref[WIDE * i : WIDE * (i + 1), :])

    wave(cov_ref, [(start(0), [], q10_ref)])
    wave(cov_ref, [(terms_of(q10_ref), [], q20_ref), (start(1), [q10_ref], q11_ref)])
    wave(
        cov_ref,
        [
            (terms_of(q20_ref), [], q30_ref),
            (terms_of(q11_ref), [q20_ref], q21_ref),
            (start(2), [q10_ref, q11_ref], q12_ref),
        ],
    )
    copy.wait()
    rotate(mean, rows_ref, q30_ref[FIRST, :], out_ref, FIRST)


def last_kernel(
    cov_ref, mean_ref, q20_ref, q30_ref, q21_ref, q12_ref, rows_hbm_ref,
    out_ref, rows_ref, q31_ref, q22_ref, q32_ref, sem,
):
    copy = pltpu.make_async_copy(rows_hbm_ref, rows_ref, sem)
    copy.start()
    mean = mean_ref[0:1, :]
    wave(
        cov_ref,
        [
            (terms_of(q21_ref), [q30_ref], q31_ref),
            (terms_of(q12_ref), [q20_ref, q21_ref], q22_ref),
        ],
    )
    copy.wait()
    rotate(mean, rows_ref, q31_ref[FIRST, :], out_ref, FIRST)
    wave(cov_ref, [(terms_of(q22_ref), [q30_ref, q31_ref], q32_ref)])
    rotate(mean, rows_ref, q32_ref[FIRST, :], out_ref, SECOND)


def in_vmem(amount):
    return [pl.BlockSpec(memory_space=pltpu.VMEM)] * amount


def stage(kernel, inputs, rows, outputs, kept, flops, name):
    amount, width = rows.shape
    terms = pltpu.VMEM((2 * WIDE, width), BF16)
    return pl.pallas_call(
        kernel,
        out_shape=outputs,
        in_specs=in_vmem(len(inputs)) + [pl.BlockSpec(memory_space=pl.ANY)],
        out_specs=in_vmem(len(outputs)),
        scratch_shapes=[pltpu.VMEM((amount, width), BF16)]
        + [terms] * kept
        + [pltpu.SemaphoreType.DMA(())],
        compiler_params=pltpu.CompilerParams(vmem_limit_bytes=VMEM_LIMIT),
        cost_estimate=pl.CostEstimate(
            flops=flops * width**3, bytes_accessed=20 * width * width, transcendentals=0
        ),
        name=name,
    )(*inputs, rows)


def moments_kernel(rows_ref, out_ref, kept_ref):
    amount, width = rows_ref.shape
    step = 256
    total = jnp.zeros((8, width), F32)
    count = jnp.zeros((8, 1), F32)
    for i in range(amount // step):
        at = slice(step * i, step * (i + 1))
        piece = rows_ref[at, :].astype(F32)
        valid = piece[:, :1] < PAD_MARK
        piece = jnp.where(valid, piece, 0.0)
        kept_ref[at, :] = piece.astype(BF16)
        total = total + jnp.sum(piece.reshape(step // 8, 8, width), axis=0)
        count = count + jnp.sum(valid.astype(F32).reshape(step // 8, 8, 1), axis=0)
    for n in range(width // 256):
        at = slice(256 * n, 256 * (n + 1))
        out_ref[at, :] = lax.dot_general(
            kept_ref[:, at], kept_ref[...], (((0,), (0,)), ((), ())), preferred_element_type=F32
        )
    line = lax.broadcasted_iota(jnp.int32, (8, width), 0)
    total = jnp.sum(total, axis=0, keepdims=True)
    count = jnp.sum(count, axis=0, keepdims=True)
    out_ref[width : width + 8, :] = jnp.where(line == 0, total, jnp.where(line == 1, count, 0.0))


def moments_of(rows):
    amount, width = rows.shape
    return pl.pallas_call(
        moments_kernel,
        out_shape=jax.ShapeDtypeStruct((width + 8, width), F32),
        in_specs=in_vmem(1),
        out_specs=pl.BlockSpec(memory_space=pltpu.VMEM),
        scratch_shapes=[pltpu.VMEM((amount, width), BF16)],
        compiler_params=pltpu.CompilerParams(vmem_limit_bytes=VMEM_LIMIT),
        name="moments",
    )(rows)


def pack_kernel(ids_ref, rows_ref, buffer_ref, place_ref):
    amount = ids_ref.shape[1]
    cell = lax.broadcasted_iota(jnp.int32, (CELLS, amount), 0)
    named = ids_ref[...] == cell
    upto = lax.broadcasted_iota(jnp.int32, (BLK, BLK), 0) <= lax.broadcasted_iota(
        jnp.int32, (BLK, BLK), 1
    )
    upto = upto.astype(BF16)
    onehot = named.astype(BF16)
    before = jnp.zeros((CELLS, 1), F32)
    goals = []
    for i in range(amount // BLK):
        at = slice(BLK * i, BLK * (i + 1))
        running = dot(onehot[:, at], upto) + before
        before = running[:, BLK - 1 :]
        goal = running - 1.0 + CAP * cell[:, at].astype(F32)
        goals.append(jnp.sum(jnp.where(named[:, at], goal, 0.0), axis=0, keepdims=True))
    goal = jnp.concatenate(goals, axis=1)
    for i in range(amount // BLK):
        at = slice(BLK * i, BLK * (i + 1))
        place_ref[at, :] = jnp.broadcast_to(goals[i], (BLK, BLK)).T
    group = 4
    slot = lax.broadcasted_iota(jnp.int32, (group * CAP, amount), 0).astype(F32)
    within = lax.broadcasted_iota(jnp.int32, (CAP, rows_ref.shape[1]), 0).astype(F32)
    for c in range(0, CELLS, group):
        hit = jnp.where(goal - float(CAP * c) == slot, 1.0, 0.0).astype(BF16)
        moved = dot(hit, rows_ref[...])
        for k in range(group):
            used = within < before[c + k : c + k + 1, :]
            part = jnp.where(used, moved[CAP * k : CAP * (k + 1), :], PAD_MARK)
            buffer_ref[c + k] = part.astype(BF16)


def unpack_kernel(place_ref, slots_ref, *refs):
    out_ref = refs[-1]
    amount, width = slots_ref.shape
    ahead = out_ref.shape[1] - width
    step = 256
    lane = lax.broadcasted_iota(jnp.int32, (step, amount), 1).astype(F32)
    for i in range(out_ref.shape[0] // step):
        at = slice(step * i, step * (i + 1))
        goal = jnp.broadcast_to(place_ref[at, :1], (step, amount))
        onehot = jnp.where(goal == lane, 1.0, 0.0).astype(BF16)
        out_ref[at, ahead:] = dot(onehot, slots_ref[...]).astype(BF16)
    first = 0
    for ready_ref in refs[:-1]:
        out_ref[:, first : first + ready_ref.shape[1]] = ready_ref[...]
        first += ready_ref.shape[1]


def pack(ids, rows):
    amount, width = rows.shape
    return pl.pallas_call(
        pack_kernel,
        out_shape=(
            jax.ShapeDtypeStruct((CELLS, CAP, width), BF16),
            jax.ShapeDtypeStruct((amount, BLK), F32),
        ),
        in_specs=in_vmem(2),
        out_specs=in_vmem(2),
        compiler_params=pltpu.CompilerParams(vmem_limit_bytes=VMEM_LIMIT),
        name="pack",
    )(ids, rows)


def unpack(place, slots, *ahead):
    width = slots.shape[1] + sum(piece.shape[1] for piece in ahead)
    return pl.pallas_call(
        unpack_kernel,
        out_shape=jax.ShapeDtypeStruct((place.shape[0], width), BF16),
        in_specs=in_vmem(2 + len(ahead)),
        out_specs=pl.BlockSpec(memory_space=pltpu.VMEM),
        compiler_params=pltpu.CompilerParams(vmem_limit_bytes=VMEM_LIMIT),
        cost_estimate=pl.CostEstimate(
            flops=2 * place.shape[0] * slots.size, bytes_accessed=4 * slots.size, transcendentals=0
        ),
        name="unpack",
    )(place, slots, *ahead)


def exchange(slots):
    width = slots.shape[-1]
    blocks = slots.reshape(CELLS, CAP, width)
    blocks = lax.all_to_all(blocks, ("z", "sub"), split_axis=0, concat_axis=0, tiled=True)
    return blocks.reshape(CELLS * CAP, width)


def body(owned, groups, rows, cell_ids, start_basis):
    width = rows.shape[1]
    swap = [(0, 1), (1, 0)]
    sub = lax.axis_index("sub")
    start = lax.dynamic_index_in_dim(start_basis, sub % owned, 0, keepdims=False)
    start_other = lax.ppermute(start, "core", swap)
    start = jnp.where(lax.axis_index("core") == sub // owned, start, start_other).T
    buffer, place = pack(cell_ids.reshape(1, -1), rows)
    received, start = lax.optimization_barrier((exchange(buffer), start))
    moments = moments_of(received)
    if groups > 1:
        moments = lax.psum(moments, "group")
    moments_other = lax.ppermute(moments, "core", swap)
    amount = received.shape[0]
    terms = jax.ShapeDtypeStruct((2 * WIDE, width), BF16)
    rotated, *state = stage(
        first_kernel,
        (moments, moments_other, start),
        received,
        [
            jax.ShapeDtypeStruct((amount, WIDE), BF16),
            jax.ShapeDtypeStruct((2 * width, width), BF16),
            jax.ShapeDtypeStruct((8, width), F32),
            terms, terms, terms, terms,
        ],
        2,
        80,
        "waves_0_to_2",
    )
    returned = exchange(rotated)
    (rotated_rest,) = stage(
        last_kernel,
        state,
        received,
        [jax.ShapeDtypeStruct((amount, width - WIDE), BF16)],
        3,
        50,
        "waves_3_to_4",
    )
    ready = unpack(place, returned)
    return unpack(place, exchange(rotated_rest), ready)


def solution(mesh):
    planes = mesh.shape["bucket"] // 2
    subs = CELLS // planes
    groups = mesh.shape["replica"] // subs
    owned = CELLS // mesh.shape["bucket"]
    fine = Mesh(mesh.devices.reshape(planes, 2, groups, subs), ("z", "core", "group", "sub"))
    row_split = P(("z", "core", "group", "sub"), None)
    return jax.shard_map(
        functools.partial(body, owned, groups),
        mesh=fine,
        in_specs=(row_split, row_split, P(("z", "core"), None, None)),
        out_specs=row_split,
        check_vma=False,
    )
```

time: 1780 us -> 253 us (0.14)
  other arithmetic: 1130 us -> 4.08 us
  matrix products: 245 us -> 0 us
  blocking collectives: 158 us -> 0 us
  local copies, waits for them, and re-layouts: 121 us -> 10.9 us
  Pallas kernels: 0 us -> 106 us
    another operation x82 -> x0, other arithmetic: 1110 us -> none  [the longest x71 733 us: orthonormal(): factor = jax.vmap(jnp.linalg.cholesky)(gram_matrix)]
    another operation x63 -> x0, matrix products: 157 us -> none  [the longest x33 98.8 us: cell_solve(): return jax.scipy.linalg.solve_triangular(factor, image.T, lower=True).T]
    all_to_all x2 -> x0, blocking collectives: 149 us -> none  [the longest x1 74.5 us: body(): lax.all_to_all(buffer, 'bucket', split_axis=0, concat_axis=1, tiled=True)]
    pallas_call x0 -> x6, Pallas kernels: none -> 106 us  [the longest x2 83.5 us: stage(): pl.pallas_call(kernel, out_shape=outputs, in_specs=in_vmem(len(inputs)) +...]
    all_to_all x1 -> x3, waiting for transfers between devices: 3.1 us -> 99.4 us  [exchange(): lax.all_to_all(blocks, ('z', 'sub'), split_axis=0, concat_axis=0, tiled=T...]
    psum x1 -> x0, waiting for transfers between devices: 93 us -> none  [body(): lax.psum((count_part, sum_part, square_part), 'replica')]
    dot_general x9 -> x0, matrix products: 88.2 us -> none  [the longest x3 40.8 us: local_gram(): jnp.einsum('cji,cjk->cik', image, image, precision=lax.Precision.HIGHEST)]
    another operation x80 -> x0, local copies, waits for them, and re-layouts: 61.4 us -> none  [the longest x58 53.5 us: cell_solve(): return jax.scipy.linalg.solve_triangular(factor, image.T, lower=True).T]
  transfers between devices with their start and end apart: 2 -> 5, of which waited for: 2 -> 4; matrix products, arithmetic and copies ran while one was open for 0% -> 4% of each run, Pallas kernels for 0% -> 15%
where the time goes in v1:
time: 253 us; the launch traced here: 250 us
  waiting for transfers between devices  109 us (43%)
  Pallas kernels  106 us (42%)
  starting transfers between devices  19.7 us (8%)
  local copies, waits for them, and re-layouts  10.9 us (4%)
  other arithmetic  4.08 us (2%)
    all_to_all x3, waiting for transfers between devices, exchange(): lax.all_to_all(blocks, ('z', 'sub'), split_axis=0, concat_axis=0, tiled=T...  99.4 us
    pallas_call x2, Pallas kernels, stage(): pl.pallas_call(kernel, out_shape=outputs, in_specs=in_vmem(len(inputs)) +...  83.5 us
    all_to_all x3, starting transfers between devices, exchange(): lax.all_to_all(blocks, ('z', 'sub'), split_axis=0, concat_axis=0, tiled=T...  19.6 us
    pallas_call x2, Pallas kernels, unpack(): pl.pallas_call(unpack_kernel, out_shape=jax.ShapeDtypeStruct((place.shape...  8.83 us
    pallas_call x1, Pallas kernels, pack(): pl.pallas_call(pack_kernel, out_shape=(jax.ShapeDtypeStruct((CELLS, CAP,...  6.82 us
    pallas_call x1, Pallas kernels, moments_of(): pl.pallas_call(moments_kernel, out_shape=jax.ShapeDtypeStruct((width + 8,...  6.73 us
    dynamic_slice x2, local copies, waits for them, and re-layouts, body(): lax.dynamic_index_in_dim(start_basis, sub % owned, 0, keepdims=False)  6.5 us
  transfers between devices with their start and end apart: 5, of which 4 were waited for; matrix products, arithmetic and copies ran while one was open for 4% of the time, Pallas kernels for 15%

profile of v1, /device:TPU:12, one launch (start us, length us, event | category | flops | bytes accessed | tf_op | source)
XLA Modules:
  0.0 249.8 jit_solution(10985134544475732400)
XLA Ops:
  0.0 6.8 %pack.1 = (bf16[16,128,768]{2,1,0:T(8,128)(2,1)}, f32[1024,128]{1,0:T(8,128)}) custom-call(s32[1,1024]{1,0:T(1,128)} %bitcast.18, bf16[1024,768]{1,0:T(8,128)(2,1)} %rows_ref.1), custom_call_target="tpu_custom_call" | custom-call | tf_op jit(solution)/shard_map/pack/pallas_call | solution.py:365
  6.8 7.2 %all-to-all-start = ((bf16[16,128,768]{2,1,0:T(8,128)(2,1)}), bf16[16,128,768]{2,1,0:T(8,128)(2,1)S(1)}, u32[]{:S(2)}, u32[]{:S(2)}) async-start(bf16[16,128,768]{2,1,0:T(8,128)(2,1)} %get-tuple-element.17), calls=%async_computation | async-start | bytes 6291456 | tf_op jit(solution)/shard_map/all_to_all | solution.py:396
  14.0 3.3 %constant_dynamic-slice_fusion = f32[1,768,768]{2,1,0:T(8,128)} fusion(f32[2,768,768]{2,1,0:T(8,128)} %param.5, s32[]{:T(128)S(6)} %select_n.26), kind=kLoop, calls=%fused_computation.1 | loop fusion | bytes 4718596 | tf_op jit(solution)/shard_map/jit(dynamic_index_in_dim)/dynamic_slice | solution.py:404
  17.3 3.2 %copy.4 = f32[1,768,768]{1,2,0:T(8,128)} copy(f32[1,768,768]{2,1,0:T(8,128)} %constant_dynamic-slice_fusion) | data formatting | bytes 4718592 | tf_op jit(solution)/shard_map/jit(dynamic_index_in_dim)/dynamic_slice | solution.py:404
  20.5 0.1 collective-permute-start
  20.6 4.8 %collective-permute-done = f32[768,768]{0,1:T(8,128)} collective-permute-done((f32[768,768]{0,1:T(8,128)}, f32[768,768]{0,1:T(8,128)}, u32[]{:S(2)}, u32[]{:S(2)}) %collective-permute-start) | collective-permute-done | bytes 2359328 | tf_op jit(solution)/shard_map/ppermute | solution.py:405
  25.4 4.1 %select_bitcast_fusion.start_ref = f32[768,768]{1,0:T(8,128)} fusion(f32[768,768]{0,1:T(8,128)} %collective-permute-done, pred[]{:T(512)S(6)} %eq.5, f32[1,768,768]{1,2,0:T(8,128)} %copy.4), kind=kLoop, calls=%fused_computation | loop fusion | flops 589824 | bytes 7077889 | tf_op jit(solution)/shard_map/transpose | solution.py:406
  29.5 54.9 %all-to-all-done = bf16[16,128,768]{2,1,0:T(8,128)(2,1)S(1)} async-done(((bf16[16,128,768]{2,1,0:T(8,128)(2,1)}), bf16[16,128,768]{2,1,0:T(8,128)(2,1)S(1)}, u32[]{:S(2)}, u32[]{:S(2)}) %all-to-all-start) | async-done | bytes 3145760 | tf_op jit(solution)/shard_map/all_to_all | solution.py:396
  84.4 0.0 copy-start
  84.4 1.6 copy-done
  86.1 6.7 %moments.1.moments_ref = f32[776,768]{1,0:T(8,128)} custom-call(bf16[2048,768]{1,0:T(8,128)(2,1)} %bitcast.10), custom_call_target="tpu_custom_call" | custom-call | tf_op jit(solution)/shard_map/moments/pallas_call | solution.py:302
  92.8 0.0 collective-permute-start.1
  92.8 4.8 %collective-permute-done.1.moments_other_ref = f32[776,768]{1,0:T(8,128)S(1)} collective-permute-done((f32[776,768]{1,0:T(8,128)}, f32[776,768]{1,0:T(8,128)S(1)}, u32[]{:S(2)}, u32[]{:S(2)}) %collective-permute-start.1) | collective-permute-done | bytes 2383904 | tf_op jit(solution)/shard_map/ppermute | solution.py:412
  97.6 0.0 copy-start.3
  97.6 1.4 copy-done.3
  99.0 49.5 %waves_0_to_2.1 = (bf16[2048,256]{1,0:T(8,128)(2,1)}, bf16[1536,768]{1,0:T(8,128)(2,1)}, f32[8,768]{1,0:T(8,128)}, bf16[512,768]{1,0:T(8,128)(2,1)}, bf16[512,76...) custom-call(f32[776,768]{1,0:T(8,128)} %moments.1.moments_ref, f32[776,768]{1,0:T(8,128)} %copy-done.3, ...), custom_call_target="tpu_custom_call" | custom-call | flops 36238786560 | bytes 11796480 | tf_op jit(solution)/shard_map/waves_0_to_2/pallas_call | solution.py:260
  148.5 5.5 %all-to-all-start.2 = ((bf16[16,128,256]{2,1,0:T(8,128)(2,1)}), bf16[16,128,256]{2,1,0:T(8,128)(2,1)S(1)}, u32[]{:S(2)}, u32[]{:S(2)}) async-start(bf16[16,128,256]{2,1,0:T(8,128)(2,1)} %bitcast.17), calls=%async_computation.2 | async-start | bytes 2097152 | tf_op jit(solution)/shard_map/all_to_all | solution.py:396
  154.0 33.9 %waves_3_to_4.1 = bf16[2048,512]{1,0:T(8,128)(2,1)} custom-call(bf16[1536,768]{1,0:T(8,128)(2,1)} %get-tuple-element.20.cov_ref, f32[8,768]{1,0:T(8,128)} %get-tuple-element.21.mean_ref, bf16[512,768]{1,0:T(8,128)(2,1)} %get-tuple-element.22.q20_ref, bf16[512,768]{1,0:T(8,128)(2,1)} %get-tuple-element.23.q30_ref, ...), custom_call_target="tpu_custom_call" | custom-call | flops 22649241600 | bytes 11796480 | tf_op jit(solution)/shard_map/waves_3_to_4/pallas_call | solution.py:260
  187.9 0.0 all-to-all-done.2
  187.9 0.0 copy-start.2
  187.9 6.9 %all-to-all-start.1 = ((bf16[16,128,512]{2,1,0:T(8,128)(2,1)}), bf16[16,128,512]{2,1,0:T(8,128)(2,1)S(1)}, u32[]{:S(2)}, u32[]{:S(2)}) async-start(bf16[16,128,512]{2,1,0:T(8,128)(2,1)} %bitcast.14), calls=%async_computation.1 | async-start | bytes 4194304 | tf_op jit(solution)/shard_map/all_to_all | solution.py:396
  194.9 0.0 copy-done.2
  194.9 3.5 %unpack.2.refs_0_ = bf16[1024,256]{1,0:T(8,128)(2,1)} custom-call(f32[1024,128]{1,0:T(8,128)} %get-tuple-element.16.place_ref, bf16[2048,256]{1,0:T(8,128)(2,1)} %bitcast.16), custom_call_target="tpu_custom_call" | custom-call | flops 1073741824 | bytes 2097152 | tf_op jit(solution)/shard_map/unpack/pallas_call | solution.py:380
  198.4 44.5 %all-to-all-done.1 = bf16[16,128,512]{2,1,0:T(8,128)(2,1)S(1)} async-done(((bf16[16,128,512]{2,1,0:T(8,128)(2,1)}), bf16[16,128,512]{2,1,0:T(8,128)(2,1)S(1)}, u32[]{:S(2)}, u32[]{:S(2)}) %all-to-all-start.1) | async-done | bytes 2097184 | tf_op jit(solution)/shard_map/all_to_all | solution.py:396
  242.9 0.0 copy-start.1
  242.9 1.3 copy-done.1
  244.2 5.3 %unpack.3 = bf16[1024,768]{1,0:T(8,128)(2,1)} custom-call(f32[1024,128]{1,0:T(8,128)} %get-tuple-element.16.place_ref, bf16[2048,512]{1,0:T(8,128)(2,1)} %bitcast.15, bf16[1024,256]{1,0:T(8,128)(2,1)} %unpack.2.refs_0_), custom_call_target="tpu_custom_call" | custom-call | flops 2147483648 | bytes 4194304 | tf_op jit(solution)/shard_map/unpack/pallas_call | solution.py:380
Async XLA Ops:
  6.8 77.6 %all-to-all-start = ((bf16[16,128,768]{2,1,0:T(8,128)(2,1)}), bf16[16,128,768]{2,1,0:T(8,128)(2,1)S(1)}, u32[]{:S(2)}, u32[]{:S(2)}) async-start(bf16[16,128,768]{2,1,0:T(8,128)(2,1)} %get-tuple-element.17), calls=%async_computation | async-start | bytes 6291456 | tf_op jit(solution)/shard_map/all_to_all | solution.py:396
  20.5 4.9 %collective-permute-start = (f32[768,768]{0,1:T(8,128)}, f32[768,768]{0,1:T(8,128)}, u32[]{:S(2)}, u32[]{:S(2)}) collective-permute-start(f32[768,768]{0,1:T(8,128)} %bitcast.13), channel_id=1, source_target_pairs={{0,4},{4,0},{1,5},{5,1},{2,6},{6,2},{3,7},{7,3},{8,12},{12,8},{9,1... | collective-permute-start | bytes 7077896 | tf_op jit(solution)/shard_map/ppermute | solution.py:405
  84.4 1.6 copy-start
  92.8 4.8 %collective-permute-start.1 = (f32[776,768]{1,0:T(8,128)}, f32[776,768]{1,0:T(8,128)S(1)}, u32[]{:S(2)}, u32[]{:S(2)}) collective-permute-start(f32[776,768]{1,0:T(8,128)} %moments.1.moments_ref), channel_id=1, source_target_pairs={{0,4},{4,0},{1,5},{5,1},{2,6},{6,2},{3,7},{7,3},{8,12},{12,8},{9,1... | collective-permute-start | bytes 7151624 | tf_op jit(solution)/shard_map/ppermute | solution.py:412
  97.6 1.4 copy-start.3
  148.5 39.4 %all-to-all-start.2 = ((bf16[16,128,256]{2,1,0:T(8,128)(2,1)}), bf16[16,128,256]{2,1,0:T(8,128)(2,1)S(1)}, u32[]{:S(2)}, u32[]{:S(2)}) async-start(bf16[16,128,256]{2,1,0:T(8,128)(2,1)} %bitcast.17), calls=%async_computation.2 | async-start | bytes 2097152 | tf_op jit(solution)/shard_map/all_to_all | solution.py:396
  187.9 6.9 %copy-start.2 = (bf16[16,128,256]{2,1,0:T(8,128)(2,1)}, bf16[16,128,256]{2,1,0:T(8,128)(2,1)S(1)}, u32[]{:S(2)}) copy-start(bf16[16,128,256]{2,1,0:T(8,128)(2,1)S(1)} %all-to-all-done.2) | copy-start | bytes 3145732
  187.9 54.9 %all-to-all-start.1 = ((bf16[16,128,512]{2,1,0:T(8,128)(2,1)}), bf16[16,128,512]{2,1,0:T(8,128)(2,1)S(1)}, u32[]{:S(2)}, u32[]{:S(2)}) async-start(bf16[16,128,512]{2,1,0:T(8,128)(2,1)} %bitcast.14), calls=%async_computation.1 | async-start | bytes 4194304 | tf_op jit(solution)/shard_map/all_to_all | solution.py:396
  242.9 1.3 copy-start.1

commit v2 on v1

--- a/solution.py
+++ b/solution.py
@@ -1,4 +1,5 @@
 import functools
+import itertools
 import jax
 import jax.numpy as jnp
 from jax import lax
@@ -39,12 +40,11 @@
     return both[:size, :] + (both[size:, :] + multiply(high, right[1]))
 
 
-def inverse_factors(squares):
+def inverse_factors(squares, beside):
     steps = BLK // SUB
     chains = range(len(squares))
     lane = lax.broadcasted_iota(jnp.int32, (SUB, BLK), 1)
     line = lax.broadcasted_iota(jnp.int32, (SUB, BLK), 0)
-    even = lax.broadcasted_iota(jnp.int32, (SUB, 2 * BLK), 0) % 2 == 0
     parts = [[square[SUB * b : SUB * (b + 1), :] for b in range(steps)] for square in squares]
     units = [[(lane == line + SUB * b).astype(F32) for b in range(steps)] for _ in chains]
     done = [[] for _ in chains]
@@ -56,9 +56,7 @@
             jnp.broadcast_to(row[:, first + k : first + k + 1], (SUB, BLK)) for k in range(SUB)
         ]
         zeros = jnp.zeros((SUB, BLK), F32)
-        return dict(
-            column=column, row=row, carry=carry, forward=carry, pivots=zeros, alpha=zeros, beta=zeros
-        )
+        return dict(column=column, row=row, carry=carry, forward=carry, pivots=zeros)
 
     def advance(state, k):
         q = k + 1
@@ -69,27 +67,25 @@
         det = head * tail - cross * side
         inverse = 1.0 / det
         pair = (line == k) | (line == q)
-        ratio_one = jnp.where(pair, 0.0, one * tail - two * side) * inverse
-        ratio_two = jnp.where(pair, 0.0, two * head - one * cross) * inverse
-
-        def clear(value, left, right):
-            return value - (left * value[k : k + 1, :] + right * value[q : q + 1, :])
+        upper, lower = line == k, line == q
+        ratio_one = jnp.where(upper, -tail, jnp.where(lower, side, one * tail - two * side)) * inverse
+        ratio_two = jnp.where(upper, cross, jnp.where(lower, -head, two * head - one * cross)) * inverse
+
+        def combined(value, left, right):
+            return left * value[k : k + 1, :] + right * value[q : q + 1, :]
+
+        def clear(value):
+            return jnp.where(pair, 0.0, value) - combined(value, ratio_one, ratio_two)
 
         for j in range(k + 2, SUB):
-            column[j] = clear(column[j], ratio_one, ratio_two)
-        state["row"] = clear(state["row"], ratio_one, ratio_two)
-        state["carry"] = clear(state["carry"], ratio_one, ratio_two)
+            column[j] = clear(column[j])
+        state["row"] = clear(state["row"])
+        state["carry"] = clear(state["carry"])
         single = 1.0 / head
-        low_one = jnp.where(line > q, ratio_one, jnp.where(line == q, side * single, 0.0))
+        low_one = jnp.where(line > q, ratio_one, jnp.where(lower, side * single, 0.0))
         low_two = jnp.where(line > q, ratio_two, 0.0)
-        state["forward"] = clear(state["forward"], low_one, low_two)
-
-        def keep(name, upper, lower):
-            state[name] = jnp.where(line == k, upper, jnp.where(line == q, lower, state[name]))
-
-        keep("pivots", head, det * single)
-        keep("alpha", tail * inverse, head * inverse)
-        keep("beta", -cross * inverse, -side * inverse)
+        state["forward"] = state["forward"] - combined(state["forward"], low_one, low_two)
+        state["pivots"] = jnp.where(upper, head, jnp.where(lower, det * single, state["pivots"]))
 
     def finish(n, b, state):
         done[n].append(state["forward"] * lax.rsqrt(state["pivots"]))
@@ -104,10 +100,7 @@
         terms = jnp.where(place == 1, pltpu.roll(low, SUB, 1), terms)
         terms = jnp.where(place == 2, pltpu.roll(high, 2 * SUB, 1), terms).astype(BF16)
         both = jnp.concatenate([state["row"], state["carry"]], axis=1)
-        swapped = jnp.where(even, pltpu.roll(both, SUB - 1, 0), pltpu.roll(both, 1, 0))
-        alpha = jnp.concatenate([state["alpha"]] * 2, axis=1)
-        beta = jnp.concatenate([state["beta"]] * 2, axis=1)
-        both_high, both_low = split(alpha * both + beta * swapped)
+        both_high, both_low = split(both)
         filled = [jnp.zeros((SUB, 2 * BLK), BF16)] * steps
         filled[b] = both_high
         filled[(b + 1) % steps] = both_high
@@ -123,13 +116,14 @@
         for k in range(0, SUB, 2):
             for state in states:
                 advance(state, k)
+            beside()
         for n in chains:
             finish(n, b, states[n])
     return [jnp.concatenate(pieces, axis=0) for pieces in done]
 
 
-def inverse_factors_wide(squares):
-    firsts = inverse_factors([square[:BLK, :BLK] for square in squares])
+def inverse_factors_wide(squares, beside):
+    firsts = inverse_factors([square[:BLK, :BLK] for square in squares], beside)
     terms = [split(first) for first in firsts]
     factors = [
         split(product(split(square[BLK:, :BLK]), term, dot_nt))
@@ -139,7 +133,8 @@
         [
             square[BLK:, BLK:] - product(factor, factor, dot_nt)
             for square, factor in zip(squares, factors)
-        ]
+        ],
+        beside,
     )
     results = []
     for first, term, factor, second in zip(firsts, terms, factors, seconds):
@@ -158,27 +153,78 @@
     return ref[FIRST, :], ref[SECOND, :]
 
 
-def wave(cov_ref, tasks):
-    width = cov_ref.shape[1]
-    images, grams = [], []
-    for source, before_refs, _ in tasks:
-        image = product(source, (cov_ref[:width, :], cov_ref[width:, :]))
-        if before_refs:
-            image_terms = split(image)
-            for before_ref in before_refs:
-                before = terms_of(before_ref)
-                along = split(product(image_terms, before, dot_nt))
-                image = image - product(along, before)
+def project(image, before_ref, exact):
+    before = terms_of(before_ref)
+    if exact:
+        return image - product(split(product(split(image), before, dot_nt)), before)
+    along = dot_nt(image.astype(BF16), before[0]).astype(BF16)
+    return image - (dot(along, before[0]) + dot(along, before[1]))
+
+
+def wave(cov_ref, tasks, beside=(), pieces=0):
+    images, grams, others = [], [], [beside]
+    for image_ref, before_refs, _, exact in tasks:
+        image = image_ref[...]
+        for before_ref in before_refs:
+            image = project(image, before_ref, exact)
         image_terms = split(image)
         images.append(image_terms)
         grams.append(product(image_terms, image_terms, dot_nt))
-    for inverse, image_terms, task in zip(inverse_factors_wide(grams), images, tasks):
-        high, low = split(product(split(inverse), image_terms))
-        task[2][FIRST, :] = high
-        task[2][SECOND, :] = low
-
-
-def rotate(mean, rows_ref, rotation, out_ref, columns):
+        if not exact:
+            others.insert(0, image_pieces(cov_ref, image_terms, image_ref))
+            pieces += 6
+    other = itertools.chain(*others)
+    ticks = itertools.count()
+    stride = max(1, BLK // max(1, pieces))
+
+    def piece():
+        if next(ticks) % stride == 0:
+            next(other, None)
+
+    inverses = inverse_factors_wide(grams, piece)
+    for _ in other:
+        pass
+    for inverse, image_terms, (image_ref, _, target_ref, exact) in zip(inverses, images, tasks):
+        rounded = inverse.astype(BF16)
+        if not exact:
+            high, low = split(image_ref[...])
+            image_ref[...] = dot(rounded, high) + dot(rounded, low)
+        if target_ref is None:
+            continue
+        if exact:
+            basis = product(split(inverse), image_terms)
+        else:
+            basis = dot(rounded, image_terms[0]) + dot(rounded, image_terms[1])
+        high, low = split(basis)
+        target_ref[FIRST, :] = high
+        target_ref[SECOND, :] = low
+
+
+def image_pieces(cov_ref, source, image_ref):
+    width = cov_ref.shape[1]
+    high, low = source
+    both = jnp.concatenate([high, low], axis=0)
+    for n in range(width // WIDE):
+        at = slice(WIDE * n, WIDE * (n + 1))
+        value = dot(both, cov_ref[:width, at])
+        yield
+        image_ref[:, at] = value[FIRST, :] + (value[SECOND, :] + dot(high, cov_ref[width:, at]))
+        yield
+
+
+def project_pieces(image_ref, before_ref):
+    width = image_ref.shape[1]
+    along = dot_nt(image_ref[...].astype(BF16), before_ref[FIRST, :]).astype(BF16)
+    yield
+    for n in range(width // WIDE):
+        at = slice(WIDE * n, WIDE * (n + 1))
+        image_ref[:, at] = image_ref[:, at] - (
+            dot(along, before_ref[FIRST, at]) + dot(along, before_ref[SECOND, at])
+        )
+        yield
+
+
+def rotate_pieces(mean, rows_ref, rotation, out_ref, columns):
     width = mean.shape[1]
     high = mean.astype(BF16)
     left = mean - high.astype(F32)
@@ -186,16 +232,23 @@
     low = (left - middle.astype(F32)).astype(BF16)
     pieces = jnp.concatenate([high, middle, low, jnp.zeros((13, width), BF16)], axis=0)
     shift = jnp.sum(dot_nt(pieces, rotation), axis=0, keepdims=True)
+    yield
     some = 512
     for n in range(rows_ref.shape[0] // some):
         at = slice(some * n, some * (n + 1))
         out_ref[at, columns] = (dot_nt(rows_ref[at, :], rotation) - shift).astype(BF16)
+        yield
+
+
+def rotate(*args):
+    for _ in rotate_pieces(*args):
+        pass
 
 
 def first_kernel(
     moments_ref, moments_other_ref, start_ref, rows_hbm_ref,
-    out_ref, cov_ref, mean_ref, q20_ref, q30_ref, q21_ref, q12_ref,
-    rows_ref, q10_ref, q11_ref, sem,
+    out_ref, cov_ref, mean_ref, q30_ref, q21_ref, image_1_ref, image_2_ref,
+    rows_ref, q10_ref, q11_ref, q20_ref, image_0_ref, sem,
 ):
     copy = pltpu.make_async_copy(rows_hbm_ref, rows_ref, sem)
     copy.start()
@@ -216,37 +269,56 @@
     def start(i):
         return split(start_ref[WIDE * i : WIDE * (i + 1), :])
 
-    wave(cov_ref, [(start(0), [], q10_ref)])
-    wave(cov_ref, [(terms_of(q10_ref), [], q20_ref), (start(1), [q10_ref], q11_ref)])
+    for _ in image_pieces(cov_ref, start(0), image_0_ref):
+        pass
+    wave(
+        cov_ref,
+        [(image_0_ref, [], q10_ref, False)],
+        itertools.chain(
+            image_pieces(cov_ref, start(1), image_1_ref),
+            image_pieces(cov_ref, start(2), image_2_ref),
+        ),
+        12,
+    )
+    wave(
+        cov_ref,
+        [(image_0_ref, [], q20_ref, False), (image_1_ref, [q10_ref], q11_ref, False)],
+        project_pieces(image_2_ref, q10_ref),
+        4,
+    )
     wave(
         cov_ref,
         [
-            (terms_of(q20_ref), [], q30_ref),
-            (terms_of(q11_ref), [q20_ref], q21_ref),
-            (start(2), [q10_ref, q11_ref], q12_ref),
+            (image_0_ref, [], q30_ref, True),
+            (image_1_ref, [q20_ref], q21_ref, False),
+            (image_2_ref, [q11_ref], None, False),
         ],
+        project_pieces(image_2_ref, q20_ref),
+        4,
     )
     copy.wait()
     rotate(mean, rows_ref, q30_ref[FIRST, :], out_ref, FIRST)
 
 
 def last_kernel(
-    cov_ref, mean_ref, q20_ref, q30_ref, q21_ref, q12_ref, rows_hbm_ref,
-    out_ref, rows_ref, q31_ref, q22_ref, q32_ref, sem,
+    cov_ref, mean_ref, q30_ref, q21_ref, image_1_ref, image_in_ref, rows_hbm_ref,
+    out_ref, rows_ref, q31_ref, q32_ref, image_2_ref, sem,
 ):
     copy = pltpu.make_async_copy(rows_hbm_ref, rows_ref, sem)
     copy.start()
     mean = mean_ref[0:1, :]
+    image_2_ref[...] = image_in_ref[...]
     wave(
         cov_ref,
-        [
-            (terms_of(q21_ref), [q30_ref], q31_ref),
-            (terms_of(q12_ref), [q20_ref, q21_ref], q22_ref),
-        ],
+        [(image_1_ref, [q30_ref], q31_ref, True), (image_2_ref, [q21_ref], None, False)],
     )
     copy.wait()
-    rotate(mean, rows_ref, q31_ref[FIRST, :], out_ref, FIRST)
-    wave(cov_ref, [(terms_of(q22_ref), [q30_ref, q31_ref], q32_ref)])
+    wave(
+        cov_ref,
+        [(image_2_ref, [q30_ref, q31_ref], q32_ref, True)],
+        rotate_pieces(mean, rows_ref, q31_ref[FIRST, :], out_ref, FIRST),
+        5,
+    )
     rotate(mean, rows_ref, q32_ref[FIRST, :], out_ref, SECOND)
 
 
@@ -256,14 +328,13 @@
 
 def stage(kernel, inputs, rows, outputs, kept, flops, name):
     amount, width = rows.shape
-    terms = pltpu.VMEM((2 * WIDE, width), BF16)
     return pl.pallas_call(
         kernel,
         out_shape=outputs,
         in_specs=in_vmem(len(inputs)) + [pl.BlockSpec(memory_space=pl.ANY)],
         out_specs=in_vmem(len(outputs)),
         scratch_shapes=[pltpu.VMEM((amount, width), BF16)]
-        + [terms] * kept
+        + kept
         + [pltpu.SemaphoreType.DMA(())],
         compiler_params=pltpu.CompilerParams(vmem_limit_bytes=VMEM_LIMIT),
         cost_estimate=pl.CostEstimate(
@@ -412,6 +483,8 @@
     moments_other = lax.ppermute(moments, "core", swap)
     amount = received.shape[0]
     terms = jax.ShapeDtypeStruct((2 * WIDE, width), BF16)
+    block = jax.ShapeDtypeStruct((WIDE, width), F32)
+    basis, image = pltpu.VMEM((2 * WIDE, width), BF16), pltpu.VMEM((WIDE, width), F32)
     rotated, *state = stage(
         first_kernel,
         (moments, moments_other, start),
@@ -420,9 +493,9 @@
             jax.ShapeDtypeStruct((amount, WIDE), BF16),
             jax.ShapeDtypeStruct((2 * width, width), BF16),
             jax.ShapeDtypeStruct((8, width), F32),
-            terms, terms, terms, terms,
+            terms, terms, block, block,
         ],
-        2,
+        [basis, basis, basis, image],
         80,
         "waves_0_to_2",
     )
@@ -432,7 +505,7 @@
         state,
         received,
         [jax.ShapeDtypeStruct((amount, width - WIDE), BF16)],
-        3,
+        [basis, basis, image],
         50,
         "waves_3_to_4",
     )

time: 253 us -> 243 us (0.960)
  Pallas kernels: 106 us -> 95 us
    pallas_call x2, Pallas kernels: 83.5 us -> 72.6 us  [stage(): pl.pallas_call(kernel, out_shape=outputs, in_specs=in_vmem(len(inputs)) +...]
  transfers between devices with their start and end apart: 5 -> 5, of which waited for: 4 -> 4; matrix products, arithmetic and copies ran while one was open for 4% -> 4% of each run, Pallas kernels for 15% -> 14%
where the time goes in v2:
time: 243 us; the launch traced here: 239 us
  waiting for transfers between devices  109 us (45%)
  Pallas kernels  95 us (39%)
  starting transfers between devices  19.8 us (8%)
  local copies, waits for them, and re-layouts  10.9 us (4%)
  other arithmetic  4.08 us (2%)
    all_to_all x3, waiting for transfers between devices, exchange(): lax.all_to_all(blocks, ('z', 'sub'), split_axis=0, concat_axis=0, tiled=T...  99.4 us
    pallas_call x2, Pallas kernels, stage(): pl.pallas_call(kernel, out_shape=outputs, in_specs=in_vmem(len(inputs)) +...  72.6 us
    all_to_all x3, starting transfers between devices, exchange(): lax.all_to_all(blocks, ('z', 'sub'), split_axis=0, concat_axis=0, tiled=T...  19.7 us
    pallas_call x2, Pallas kernels, unpack(): pl.pallas_call(unpack_kernel, out_shape=jax.ShapeDtypeStruct((place.shape...  8.83 us
    pallas_call x1, Pallas kernels, pack(): pl.pallas_call(pack_kernel, out_shape=(jax.ShapeDtypeStruct((CELLS, CAP,...  6.82 us
    pallas_call x1, Pallas kernels, moments_of(): pl.pallas_call(moments_kernel, out_shape=jax.ShapeDtypeStruct((width + 8,...  6.74 us
    dynamic_slice x2, local copies, waits for them, and re-layouts, body(): lax.dynamic_index_in_dim(start_basis, sub % owned, 0, keepdims=False)  6.55 us
  transfers between devices with their start and end apart: 5, of which 4 were waited for; matrix products, arithmetic and copies ran while one was open for 4% of the time, Pallas kernels for 14%

profile of v2, /device:TPU:12, one launch (start us, length us, event | category | flops | bytes accessed | tf_op | source)
XLA Modules:
  0.0 239.3 jit_solution(1698302418855188715)
XLA Ops:
  0.0 6.8 %pack.1 = (bf16[16,128,768]{2,1,0:T(8,128)(2,1)}, f32[1024,128]{1,0:T(8,128)}) custom-call(s32[1,1024]{1,0:T(1,128)} %bitcast.18, bf16[1024,768]{1,0:T(8,128)(2,1)} %rows_ref.1), custom_call_target="tpu_custom_call" | custom-call | tf_op jit(solution)/shard_map/pack/pallas_call | solution.py:436
  6.8 7.2 %all-to-all-start = ((bf16[16,128,768]{2,1,0:T(8,128)(2,1)}), bf16[16,128,768]{2,1,0:T(8,128)(2,1)S(1)}, u32[]{:S(2)}, u32[]{:S(2)}) async-start(bf16[16,128,768]{2,1,0:T(8,128)(2,1)} %get-tuple-element.17), calls=%async_computation | async-start | bytes 6291456 | tf_op jit(solution)/shard_map/all_to_all | solution.py:467
  14.0 3.3 %constant_dynamic-slice_fusion = f32[1,768,768]{2,1,0:T(8,128)} fusion(f32[2,768,768]{2,1,0:T(8,128)} %param.5, s32[]{:T(128)S(6)} %select_n.26), kind=kLoop, calls=%fused_computation.1 | loop fusion | bytes 4718596 | tf_op jit(solution)/shard_map/jit(dynamic_index_in_dim)/dynamic_slice | solution.py:475
  17.3 3.3 %copy.4 = f32[1,768,768]{1,2,0:T(8,128)} copy(f32[1,768,768]{2,1,0:T(8,128)} %constant_dynamic-slice_fusion) | data formatting | bytes 4718592 | tf_op jit(solution)/shard_map/jit(dynamic_index_in_dim)/dynamic_slice | solution.py:475
  20.5 0.1 collective-permute-start
  20.6 4.8 %collective-permute-done = f32[768,768]{0,1:T(8,128)} collective-permute-done((f32[768,768]{0,1:T(8,128)}, f32[768,768]{0,1:T(8,128)}, u32[]{:S(2)}, u32[]{:S(2)}) %collective-permute-start) | collective-permute-done | bytes 2359328 | tf_op jit(solution)/shard_map/ppermute | solution.py:476
  25.5 4.1 %select_bitcast_fusion.start_ref = f32[768,768]{1,0:T(8,128)} fusion(f32[768,768]{0,1:T(8,128)} %collective-permute-done, pred[]{:T(512)S(6)} %eq.5, f32[1,768,768]{1,2,0:T(8,128)} %copy.4), kind=kLoop, calls=%fused_computation | loop fusion | flops 589824 | bytes 7077889 | tf_op jit(solution)/shard_map/transpose | solution.py:477
  29.6 54.9 %all-to-all-done = bf16[16,128,768]{2,1,0:T(8,128)(2,1)S(1)} async-done(((bf16[16,128,768]{2,1,0:T(8,128)(2,1)}), bf16[16,128,768]{2,1,0:T(8,128)(2,1)S(1)}, u32[]{:S(2)}, u32[]{:S(2)}) %all-to-all-start) | async-done | bytes 3145760 | tf_op jit(solution)/shard_map/all_to_all | solution.py:467
  84.5 0.0 copy-start
  84.5 1.6 copy-done
  86.1 6.7 %moments.1.moments_ref = f32[776,768]{1,0:T(8,128)} custom-call(bf16[2048,768]{1,0:T(8,128)(2,1)} %bitcast.10), custom_call_target="tpu_custom_call" | custom-call | tf_op jit(solution)/shard_map/moments/pallas_call | solution.py:373
  92.8 0.0 collective-permute-start.1
  92.8 4.8 %collective-permute-done.1.moments_other_ref = f32[776,768]{1,0:T(8,128)S(1)} collective-permute-done((f32[776,768]{1,0:T(8,128)}, f32[776,768]{1,0:T(8,128)S(1)}, u32[]{:S(2)}, u32[]{:S(2)}) %collective-permute-start.1) | collective-permute-done | bytes 2383904 | tf_op jit(solution)/shard_map/ppermute | solution.py:483
  97.6 0.0 copy-start.3
  97.6 1.4 copy-done.3
  99.0 43.7 %waves_0_to_2.1 = (bf16[2048,256]{1,0:T(8,128)(2,1)}, bf16[1536,768]{1,0:T(8,128)(2,1)}, f32[8,768]{1,0:T(8,128)}, bf16[512,768]{1,0:T(8,128)(2,1)}, bf16[512,76...) custom-call(f32[776,768]{1,0:T(8,128)} %moments.1.moments_ref, f32[776,768]{1,0:T(8,128)} %copy-done.3, ...), custom_call_target="tpu_custom_call" | custom-call | flops 36238786560 | bytes 11796480 | tf_op jit(solution)/shard_map/waves_0_to_2/pallas_call | solution.py:331
  142.7 5.7 %all-to-all-start.2 = ((bf16[16,128,256]{2,1,0:T(8,128)(2,1)}), bf16[16,128,256]{2,1,0:T(8,128)(2,1)S(1)}, u32[]{:S(2)}, u32[]{:S(2)}) async-start(bf16[16,128,256]{2,1,0:T(8,128)(2,1)} %bitcast.17), calls=%async_computation.2 | async-start | bytes 2097152 | tf_op jit(solution)/shard_map/all_to_all | solution.py:467
  148.4 28.9 %waves_3_to_4.1 = bf16[2048,512]{1,0:T(8,128)(2,1)} custom-call(bf16[1536,768]{1,0:T(8,128)(2,1)} %get-tuple-element.20.cov_ref, f32[8,768]{1,0:T(8,128)} %get-tuple-element.21.mean_ref, bf16[512,768]{1,0:T(8,128)(2,1)} %get-tuple-element.22.q30_ref, bf16[512,768]{1,0:T(8,128)(2,1)} %get-tuple-element.23.q21_ref, f32[256,768]{1,0:T(8,128)} %get-tuple-element.24.image_1_ref, ...), custom_call_target="tpu_custom_call" | custom-call | flops 22649241600 | bytes 11796480 | tf_op jit(solution)/shard_map/waves_3_to_4/pallas_call | solution.py:331
  177.3 0.0 all-to-all-done.2
  177.3 0.0 copy-start.2
  177.3 6.9 %all-to-all-start.1 = ((bf16[16,128,512]{2,1,0:T(8,128)(2,1)}), bf16[16,128,512]{2,1,0:T(8,128)(2,1)S(1)}, u32[]{:S(2)}, u32[]{:S(2)}) async-start(bf16[16,128,512]{2,1,0:T(8,128)(2,1)} %bitcast.14), calls=%async_computation.1 | async-start | bytes 4194304 | tf_op jit(solution)/shard_map/all_to_all | solution.py:467
  184.2 0.0 copy-done.2
  184.2 3.5 %unpack.2.refs_0_ = bf16[1024,256]{1,0:T(8,128)(2,1)} custom-call(f32[1024,128]{1,0:T(8,128)} %get-tuple-element.16.place_ref, bf16[2048,256]{1,0:T(8,128)(2,1)} %bitcast.16), custom_call_target="tpu_custom_call" | custom-call | flops 1073741824 | bytes 2097152 | tf_op jit(solution)/shard_map/unpack/pallas_call | solution.py:451
  187.7 44.5 %all-to-all-done.1 = bf16[16,128,512]{2,1,0:T(8,128)(2,1)S(1)} async-done(((bf16[16,128,512]{2,1,0:T(8,128)(2,1)}), bf16[16,128,512]{2,1,0:T(8,128)(2,1)S(1)}, u32[]{:S(2)}, u32[]{:S(2)}) %all-to-all-start.1) | async-done | bytes 2097184 | tf_op jit(solution)/shard_map/all_to_all | solution.py:467
  232.2 0.0 copy-start.1
  232.2 1.3 copy-done.1
  233.5 5.3 %unpack.3 = bf16[1024,768]{1,0:T(8,128)(2,1)} custom-call(f32[1024,128]{1,0:T(8,128)} %get-tuple-element.16.place_ref, bf16[2048,512]{1,0:T(8,128)(2,1)} %bitcast.15, bf16[1024,256]{1,0:T(8,128)(2,1)} %unpack.2.refs_0_), custom_call_target="tpu_custom_call" | custom-call | flops 2147483648 | bytes 4194304 | tf_op jit(solution)/shard_map/unpack/pallas_call | solution.py:451
Async XLA Ops:
  6.8 77.6 %all-to-all-start = ((bf16[16,128,768]{2,1,0:T(8,128)(2,1)}), bf16[16,128,768]{2,1,0:T(8,128)(2,1)S(1)}, u32[]{:S(2)}, u32[]{:S(2)}) async-start(bf16[16,128,768]{2,1,0:T(8,128)(2,1)} %get-tuple-element.17), calls=%async_computation | async-start | bytes 6291456 | tf_op jit(solution)/shard_map/all_to_all | solution.py:467
  20.5 4.9 %collective-permute-start = (f32[768,768]{0,1:T(8,128)}, f32[768,768]{0,1:T(8,128)}, u32[]{:S(2)}, u32[]{:S(2)}) collective-permute-start(f32[768,768]{0,1:T(8,128)} %bitcast.13), channel_id=1, source_target_pairs={{0,4},{4,0},{1,5},{5,1},{2,6},{6,2},{3,7},{7,3},{8,12},{12,8},{9,1... | collective-permute-start | bytes 7077896 | tf_op jit(solution)/shard_map/ppermute | solution.py:476
  84.5 1.6 copy-start
  92.8 4.8 %collective-permute-start.1 = (f32[776,768]{1,0:T(8,128)}, f32[776,768]{1,0:T(8,128)S(1)}, u32[]{:S(2)}, u32[]{:S(2)}) collective-permute-start(f32[776,768]{1,0:T(8,128)} %moments.1.moments_ref), channel_id=1, source_target_pairs={{0,4},{4,0},{1,5},{5,1},{2,6},{6,2},{3,7},{7,3},{8,12},{12,8},{9,1... | collective-permute-start | bytes 7151624 | tf_op jit(solution)/shard_map/ppermute | solution.py:483
  97.6 1.4 copy-start.3
  142.7 34.6 %all-to-all-start.2 = ((bf16[16,128,256]{2,1,0:T(8,128)(2,1)}), bf16[16,128,256]{2,1,0:T(8,128)(2,1)S(1)}, u32[]{:S(2)}, u32[]{:S(2)}) async-start(bf16[16,128,256]{2,1,0:T(8,128)(2,1)} %bitcast.17), calls=%async_computation.2 | async-start | bytes 2097152 | tf_op jit(solution)/shard_map/all_to_all | solution.py:467
  177.3 6.9 %copy-start.2 = (bf16[16,128,256]{2,1,0:T(8,128)(2,1)}, bf16[16,128,256]{2,1,0:T(8,128)(2,1)S(1)}, u32[]{:S(2)}) copy-start(bf16[16,128,256]{2,1,0:T(8,128)(2,1)S(1)} %all-to-all-done.2) | copy-start | bytes 3145732
  177.3 54.9 %all-to-all-start.1 = ((bf16[16,128,512]{2,1,0:T(8,128)(2,1)}), bf16[16,128,512]{2,1,0:T(8,128)(2,1)S(1)}, u32[]{:S(2)}, u32[]{:S(2)}) async-start(bf16[16,128,512]{2,1,0:T(8,128)(2,1)} %bitcast.14), calls=%async_computation.1 | async-start | bytes 4194304 | tf_op jit(solution)/shard_map/all_to_all | solution.py:467
  232.2 1.3 copy-start.1
